TPU v7x, 32 devices: a whole 2x2x4 slice. The times are simulated.
32 devices in a mesh: section: 4 (over z), ctx: 4 (over x, core), dp: 2 (over y).
Axes of the slice: x: 2, y: 2, z: 4, core: 2. Of those that a mesh axis runs over, the one named last changes fastest.
Arguments:
- stream: bfloat16 [4, 256, 8192], P('section', 'dp', 'ctx'), may hold values from -6 to 6
- norm_gain: float32 [4, 8192], P('section', 'ctx'), may hold values from 0.5 to 2
- w_router: bfloat16 [4, 8192], P('section', 'ctx'), may hold values from -0.0625 to 0.0625
- w_gate: bfloat16 [4, 8192, 14336], P('section', 'ctx', 'dp'), may hold values from -0.0625 to 0.0625
- w_up: bfloat16 [4, 8192, 14336], P('section', 'ctx', 'dp'), may hold values from -0.0625 to 0.0625
- w_down: bfloat16 [4, 14336, 8192], P('section', 'dp', 'ctx'), may hold values from -0.046875 to 0.046875
- keep_rows: int32 [2, 4, 2, 32], P(None, 'section', 'dp'), may hold values from -1 to 127, as said below
Outputs:
- advanced: bfloat16 [4, 256, 8192], P('section', 'dp', 'ctx')
Inputs may be any that keep to these rules, and one draw needn't show every extreme that they name: `keep_rows`: each list holds distinct row indices first, then -1 in its empty slots. Over the 2 lists of one tick and section exactly 32 rows are kept; in each tick and section some list is full and some is empty.
All inputs are finite; a program needn't handle non-finite values.
Results may differ from a plain program's by a relative error of at most 0.005.
Values may be sent and summed in bfloat16 or wider, within the bound.
A program may use at most 192 MiB of HBM per device.

v0:
```python
import jax
import jax.numpy as jnp
from jax import lax
from jax.sharding import PartitionSpec as P

D = 8192
eps = 1e-05


def from_behind(value, axis, steps):
    count = lax.axis_size(axis)
    pairs = [(source, (source + steps) % count) for source in range(count)]
    return lax.ppermute(value, axis, pairs)


def hidden_block(normed, w_gate, w_up, w_down):
    row_piece = lax.all_gather(normed, "dp", axis=0, tiled=True)
    gate_part = jnp.dot(row_piece, w_gate, preferred_element_type=jnp.float32)
    up_part = jnp.dot(row_piece, w_up, preferred_element_type=jnp.float32)
    partial_value = jnp.stack([gate_part, up_part], axis=1)
    summed = lax.psum(partial_value, "ctx")
    hidden = (jax.nn.silu(summed[:, 0]) * summed[:, 1]).astype(jnp.bfloat16)
    return lax.psum_scatter(
        jnp.dot(hidden, w_down, preferred_element_type=jnp.float32).astype(jnp.bfloat16),
        "dp",
        scatter_dimension=0,
        tiled=True,
    ).astype(jnp.float32)


def routed_layer(stream, keep_list, gain_row, router, w_gate, w_up, w_down):
    is_kept = keep_list >= 0
    picked = jnp.take(stream, jnp.maximum(keep_list, 0), axis=0)
    rows_wide = picked.astype(jnp.float32)
    squares = jnp.sum(rows_wide * rows_wide, axis=1)
    logits = jnp.sum(rows_wide * router.astype(jnp.float32)[None, :], axis=1)
    squares, logits = lax.psum((squares, logits), "ctx")
    scaling = lax.rsqrt(squares / D + eps)
    normed = jnp.where(
        is_kept[:, None], rows_wide * scaling[:, None] * gain_row[None, :], 0.0
    ).astype(jnp.bfloat16)
    update = hidden_block(normed, w_gate, w_up, w_down)
    new_rows = (rows_wide + jax.nn.sigmoid(logits)[:, None] * update).astype(jnp.bfloat16)
    target = jnp.where(is_kept, keep_list, stream.shape[0])
    return stream.at[target].set(new_rows, mode="drop")


def local(stream, norm_gain, w_router, w_gate, w_up, w_down, keep_rows):
    first_pass = routed_layer(
        stream[0], keep_rows[0, 0, 0], norm_gain[0], w_router[0], w_gate[0], w_up[0], w_down[0]
    )
    passed = from_behind(first_pass, "section", 1)
    second_pass = routed_layer(
        passed, keep_rows[1, 0, 0], norm_gain[0], w_router[0], w_gate[0], w_up[0], w_down[0]
    )
    section_place = lax.axis_index("section")
    result = jnp.where(section_place == 0, passed, second_pass)
    return result[None]


def solution(mesh):
    return jax.shard_map(
        local,
        mesh=mesh,
        in_specs=(
            P("section", "dp", "ctx"),
            P("section", "ctx"),
            P("section", "ctx"),
            P("section", "ctx", "dp"),
            P("section", "ctx", "dp"),
            P("section", "dp", "ctx"),
            P(None, "section", "dp", None),
        ),
        out_specs=P("section", "dp", "ctx"),
        check_vma=False,
    )
```

profile of v0, /device:TPU:0, one launch (start us, length us, event | category | flops | bytes accessed | tf_op | source)
XLA Modules:
  0.0 325.9 jit_solution(13672440571319732338)
XLA Ops:
  6.5 1.0 copy.13
  8.9 0.7 mul.113
  10.5 8.3 %all-reduce.1 = (f32[32]{0:T(128)S(1)}, f32[32]{0:T(128)S(1)}) all-reduce(f32[32]{0:T(128)S(1)} %get-tuple-element.9, f32[32]{0:T(128)S(1)} %get-tuple-element.8), channel_id=1, replica_groups=mesh['section'=4,'ctx'=4,'dp'=2] {'ctx'}, use_global_device_ids=true, to_apply=%region_3.5 | all-reduce | flops 64 | bytes 512 | tf_op jit(solution)/shard_map/psum | solution.py:37
  18.9 0.8 fusion.40
  19.7 5.6 %all_gather.6 = bf16[64,2048]{1,0:T(8,128)(2,1)S(1)} all-gather(bf16[32,2048]{1,0:T(8,128)(2,1)S(1)} %fusion.40), channel_id=1, replica_groups=mesh['section'=4,'ctx'=4,'dp'=2] {'dp'}, dimensions={0}, use_global_device_ids=true | all-gather | bytes 393216 | tf_op jit(solution)/shard_map/all_gather | solution.py:17
  25.4 12.0 %fusion.12 = f32[64,1,7168]{2,0,1:T(8,128)S(1)} fusion(bf16[64,2048]{1,0:T(8,128)(2,1)S(1)} %all_gather.6, bf16[1,2048,7168]{2,1,0:T(8,128)(2,1)} %param.12), kind=kOutput, calls=%fused_computation.16 | convolution fusion | flops 1879048192 | bytes 31457280 | tf_op jit(solution)/shard_map/dot_general | solution.py:18
  37.3 12.0 %fusion.18 = f32[64,1,7168]{2,0,1:T(8,128)S(1)} fusion(bf16[64,2048]{1,0:T(8,128)(2,1)S(1)} %all_gather.6, bf16[1,2048,7168]{2,1,0:T(8,128)(2,1)} %param.13), kind=kOutput, calls=%fused_computation.18 | convolution fusion | flops 1879048192 | bytes 31457280 | tf_op jit(solution)/shard_map/dot_general | solution.py:19
  49.3 2.1 pad_maximum_fusion
  51.5 77.4 %all-reduce.5.cloned.1.call-done = f32[64,2,7168]{2,0,1:T(8,128)} async-done(((f32[64,2,7168]{2,0,1:T(8,128)}), f32[64,2,7168]{2,0,1:T(8,128)}) %all-reduce.5.cloned.1.call-update) | async-done | bytes 3670032 | tf_op jit(solution)/shard_map/psum | solution.py:21
  128.9 16.4 %fusion.24 = bf16[64,2048]{1,0:T(8,128)(2,1)} fusion(bf16[1,7168,2048]{2,1,0:T(8,128)(2,1)} %param.14, f32[64,2,7168]{2,0,1:T(8,128)} %all-reduce.5.cloned.1.call-done), kind=kOutput, calls=%fused_computation.22 | convolution fusion | flops 1881931776 | bytes 33292288 | tf_op jit(solution)/shard_map/dot_general | solution.py:24
  145.4 11.9 %reduce-scatter.3.cloned.1.call-done = bf16[32,2048]{1,0:T(8,128)(2,1)} async-done(((bf16[64,2048]{1,0:T(8,128)(2,1)}), bf16[32,2048]{1,0:T(8,128)(2,1)}) %reduce-scatter.3.cloned.1.call-update) | async-done | bytes 131088 | tf_op jit(solution)/shard_map/reduce_scatter | solution.py:23
  157.3 1.6 scatter_custom_fusion
  158.9 1.5 collective-permute-start
  160.4 14.0 %collective-permute-done = bf16[128,2048]{1,0:T(8,128)(2,1)S(1)} collective-permute-done((bf16[128,2048]{1,0:T(8,128)(2,1)S(1)}, bf16[128,2048]{1,0:T(8,128)(2,1)S(1)}, u32[]{:S(2)}, u32[]{:S(2)}) %collective-permute-start) | collective-permute-done | bytes 524320 | tf_op jit(solution)/shard_map/ppermute | solution.py:13
  175.3 5.7 %all-reduce = (f32[32]{0:T(128)S(1)}, f32[32]{0:T(128)S(1)}) all-reduce(f32[32]{0:T(128)S(1)} %get-tuple-element.7, f32[32]{0:T(128)S(1)} %get-tuple-element.6), channel_id=1, replica_groups=mesh['section'=4,'ctx'=4,'dp'=2] {'ctx'}, use_global_device_ids=true, to_apply=%region_10.12 | all-reduce | flops 64 | bytes 512 | tf_op jit(solution)/shard_map/psum | solution.py:37
  181.1 6.1 %all_gather.7 = bf16[64,2048]{1,0:T(8,128)(2,1)S(1)} all-gather(bf16[32,2048]{1,0:T(8,128)(2,1)S(1)} %fusion.46), channel_id=1, replica_groups=mesh['section'=4,'ctx'=4,'dp'=2] {'dp'}, dimensions={0}, use_global_device_ids=true | all-gather | bytes 393216 | tf_op jit(solution)/shard_map/all_gather | solution.py:17
  187.2 12.0 %fusion.15 = f32[64,1,7168]{2,0,1:T(8,128)S(1)} fusion(bf16[64,2048]{1,0:T(8,128)(2,1)S(1)} %all_gather.7, bf16[1,2048,7168]{2,1,0:T(8,128)(2,1)} %param.12), kind=kOutput, calls=%fused_computation.17 | convolution fusion | flops 1879048192 | bytes 31457280 | tf_op jit(solution)/shard_map/dot_general | solution.py:18
  199.2 12.0 %fusion.21 = f32[64,1,7168]{2,0,1:T(8,128)S(1)} fusion(bf16[64,2048]{1,0:T(8,128)(2,1)S(1)} %all_gather.7, bf16[1,2048,7168]{2,1,0:T(8,128)(2,1)} %param.13), kind=kOutput, calls=%fused_computation.19 | convolution fusion | flops 1879048192 | bytes 31457280 | tf_op jit(solution)/shard_map/dot_general | solution.py:19
  211.2 2.1 pad_maximum_fusion.1
  213.4 75.2 %all-reduce.7.cloned.1.call-done = f32[64,2,7168]{2,0,1:T(8,128)} async-done(((f32[64,2,7168]{2,0,1:T(8,128)}), f32[64,2,7168]{2,0,1:T(8,128)}) %all-reduce.7.cloned.1.call-update) | async-done | bytes 3670032 | tf_op jit(solution)/shard_map/psum | solution.py:21
  288.6 16.4 %fusion.27 = bf16[64,2048]{1,0:T(8,128)(2,1)} fusion(bf16[1,7168,2048]{2,1,0:T(8,128)(2,1)} %param.14, f32[64,2,7168]{2,0,1:T(8,128)} %all-reduce.7.cloned.1.call-done), kind=kOutput, calls=%fused_computation.23 | convolution fusion | flops 1881931776 | bytes 33292288 | tf_op jit(solution)/shard_map/dot_general | solution.py:24
  305.1 11.9 %reduce-scatter.5.cloned.1.call-done = bf16[32,2048]{1,0:T(8,128)(2,1)} async-done(((bf16[64,2048]{1,0:T(8,128)(2,1)}), bf16[32,2048]{1,0:T(8,128)(2,1)}) %reduce-scatter.5.cloned.1.call-update) | async-done | bytes 131088 | tf_op jit(solution)/shard_map/reduce_scatter | solution.py:23
  316.9 1.6 scatter_custom_fusion.1
  318.5 0.9 select_bitcast_fusion
  (27 shorter events, 3.5 us)
Async XLA Ops:
  6.5 122.4 %all-reduce.5.cloned.1.call-start = ((), (), s32[]{:S(2)}) async-start(), calls=%async_computation.2 | async-start | bytes 7340032 | tf_op jit(solution)/shard_map/psum | solution.py:21
  51.5 93.9 %copy-start.1 = (s32[2,1,1,32]{3,2,1,0:T(1,128)S(1)}, s32[2,1,1,32]{3,2,1,0:T(1,128)}, u32[]{:S(2)}) copy-start(s32[2,1,1,32]{3,2,1,0:T(1,128)} %param.15) | copy-start | bytes 772
  51.5 129.5 %copy-start = (f32[1,2048]{1,0:T(1,128)S(1)}, f32[1,2048]{1,0:T(1,128)}, u32[]{:S(2)}) copy-start(f32[1,2048]{1,0:T(1,128)} %param.10) | copy-start | bytes 24580
  51.5 105.8 %reduce-scatter.3.cloned.1.call-start = ((), (), s32[]{:S(2)}) async-start(), calls=%async_computation.3 | async-start | bytes 393216 | tf_op jit(solution)/shard_map/reduce_scatter | solution.py:23
  145.3 143.3 %all-reduce.7.cloned.1.call-start = ((), (), s32[]{:S(2)}) async-start(), calls=%async_computation.4 | async-start | bytes 7340032 | tf_op jit(solution)/shard_map/psum | solution.py:21
  158.9 15.5 %collective-permute-start = (bf16[128,2048]{1,0:T(8,128)(2,1)S(1)}, bf16[128,2048]{1,0:T(8,128)(2,1)S(1)}, u32[]{:S(2)}, u32[]{:S(2)}) collective-permute-start(bf16[128,2048]{1,0:T(8,128)(2,1)S(1)} %scatter_custom_fusion), channel_id=1, source_target_pairs={{0,8},{8,16},{16,24},{24,0},{1,9},{9,17},{17,25},{25,1},{2,10},{10... | collective-permute-start | bytes 1572872 | tf_op jit(solution)/shard_map/ppermute | solution.py:13
  213.3 103.6 %reduce-scatter.5.cloned.1.call-start = ((), (), s32[]{:S(2)}) async-start(), calls=%async_computation.5 | async-start | bytes 393216 | tf_op jit(solution)/shard_map/reduce_scatter | solution.py:23
Sparse Core Ops, SparseCore 0:
  51.6 77.3 all-reduce.4
  145.5 11.7 reduce-scatter.2
  213.4 75.1 all-reduce.6
  305.1 11.7 reduce-scatter.4
where the time goes:
time: 326 us
  waiting for transfers between devices  190 us (58%)
  matrix products  80.7 us (25%)
  blocking collectives  25.8 us (8%)
  between operations  13.3 us (4%)
  other arithmetic  11.7 us (4%)
    psum x2, waiting for transfers between devices, hidden_block(): summed = lax.psum(partial_value, 'ctx')  153 us
    dot_general x2, matrix products, hidden_block(): jnp.dot(hidden, w_down, preferred_element_type=jnp.float32)  32.8 us
    dot_general x2, matrix products, hidden_block(): up_part = jnp.dot(row_piece, w_up, preferred_element_type=jnp.float32)  24 us
    dot_general x2, matrix products, hidden_block(): gate_part = jnp.dot(row_piece, w_gate, preferred_element_type=jnp.float32)  24 us
    reduce_scatter x2, waiting for transfers between devices, hidden_block(): lax.psum_scatter(jnp.dot(hidden, w_down, preferred_element_type=jnp.float...  23.7 us
    psum x2, blocking collectives, routed_layer(): squares, logits = lax.psum((squares, logits), 'ctx')  14 us
    ppermute x1, waiting for transfers between devices, from_behind(): return lax.ppermute(value, axis, pairs)  14 us
    all_gather x2, blocking collectives, hidden_block(): row_piece = lax.all_gather(normed, 'dp', axis=0, tiled=True)  11.7 us
  transfers between devices with their start and end apart: 5, of which 5 were waited for; matrix products, arithmetic and copies ran while one was open for 0% of the time, Pallas kernels for 0%

commit v1 on v0

--- a/solution.py
+++ b/solution.py
@@ -18,7 +18,8 @@
     gate_part = jnp.dot(row_piece, w_gate, preferred_element_type=jnp.float32)
     up_part = jnp.dot(row_piece, w_up, preferred_element_type=jnp.float32)
     partial_value = jnp.stack([gate_part, up_part], axis=1)
-    summed = lax.psum(partial_value, "ctx")
+    shards = lax.all_gather(partial_value, "ctx")
+    summed = jnp.sum(shards, axis=0)
     hidden = (jax.nn.silu(summed[:, 0]) * summed[:, 1]).astype(jnp.bfloat16)
     return lax.psum_scatter(
         jnp.dot(hidden, w_down, preferred_element_type=jnp.float32).astype(jnp.bfloat16),

time: 326 us -> 377 us (1.16)
  waiting for transfers between devices: 190 us -> 224 us
  other arithmetic: 11.7 us -> 28.4 us
    all_gather x0 -> x2, waiting for transfers between devices: none -> 187 us  [hidden_block(): shards = lax.all_gather(partial_value, 'ctx')]
    psum x2 -> x0, waiting for transfers between devices: 153 us -> none  [hidden_block(): summed = lax.psum(partial_value, 'ctx')]
    reduce_sum x0 -> x2, other arithmetic: none -> 16.9 us  [hidden_block(): summed = jnp.sum(shards, axis=0)]
where the time goes in v1:
time: 377 us
  waiting for transfers between devices  224 us (59%)
  matrix products  80.8 us (21%)
  other arithmetic  28.4 us (8%)
  blocking collectives  25.8 us (7%)
  between operations  13.3 us (4%)
    all_gather x2, waiting for transfers between devices, hidden_block(): shards = lax.all_gather(partial_value, 'ctx')  187 us
    dot_general x2, matrix products, hidden_block(): jnp.dot(hidden, w_down, preferred_element_type=jnp.float32)  32.8 us
    dot_general x2, matrix products, hidden_block(): up_part = jnp.dot(row_piece, w_up, preferred_element_type=jnp.float32)  24 us
    dot_general x2, matrix products, hidden_block(): gate_part = jnp.dot(row_piece, w_gate, preferred_element_type=jnp.float32)  24 us
    reduce_scatter x2, waiting for transfers between devices, hidden_block(): lax.psum_scatter(jnp.dot(hidden, w_down, preferred_element_type=jnp.float...  23.5 us
    reduce_sum x2, other arithmetic, hidden_block(): summed = jnp.sum(shards, axis=0)  16.9 us
    psum x2, blocking collectives, routed_layer(): squares, logits = lax.psum((squares, logits), 'ctx')  14 us
    ppermute x1, waiting for transfers between devices, from_behind(): return lax.ppermute(value, axis, pairs)  14 us
  transfers between devices with their start and end apart: 5, of which 5 were waited for; matrix products, arithmetic and copies ran while one was open for 0% of the time, Pallas kernels for 0%

profile of v1, /device:TPU:0, one launch (start us, length us, event | category | flops | bytes accessed | tf_op | source)
XLA Modules:
  0.0 376.6 jit_solution(18255667798704496331)
XLA Ops:
  6.5 1.0 copy.11
  10.5 8.3 %all-reduce.1 = (f32[32]{0:T(128)S(1)}, f32[32]{0:T(128)S(1)}) all-reduce(f32[32]{0:T(128)S(1)} %get-tuple-element.9, f32[32]{0:T(128)S(1)} %get-tuple-element.8), channel_id=1, replica_groups=mesh['section'=4,'ctx'=4,'dp'=2] {'ctx'}, use_global_device_ids=true, to_apply=%region_3.5 | all-reduce | flops 64 | bytes 512 | tf_op jit(solution)/shard_map/psum | solution.py:38
  19.7 5.6 %all_gather.18 = bf16[64,2048]{1,0:T(8,128)(2,1)S(1)} all-gather(bf16[32,2048]{1,0:T(8,128)(2,1)S(1)} %fusion.40), channel_id=1, replica_groups=mesh['section'=4,'ctx'=4,'dp'=2] {'dp'}, dimensions={0}, use_global_device_ids=true | all-gather | bytes 393216 | tf_op jit(solution)/shard_map/all_gather | solution.py:17
  25.4 12.0 %fusion.12 = f32[64,1,7168]{2,0,1:T(8,128)S(1)} fusion(bf16[64,2048]{1,0:T(8,128)(2,1)S(1)} %all_gather.18, bf16[1,2048,7168]{2,1,0:T(8,128)(2,1)} %param.12), kind=kOutput, calls=%fused_computation.16 | convolution fusion | flops 1879048192 | bytes 31457280 | tf_op jit(solution)/shard_map/dot_general | solution.py:18
  37.3 12.0 %fusion.18 = f32[64,1,7168]{2,0,1:T(8,128)S(1)} fusion(bf16[64,2048]{1,0:T(8,128)(2,1)S(1)} %all_gather.18, bf16[1,2048,7168]{2,1,0:T(8,128)(2,1)} %param.13), kind=kOutput, calls=%fused_computation.18 | convolution fusion | flops 1879048192 | bytes 31457280 | tf_op jit(solution)/shard_map/dot_general | solution.py:19
  49.3 2.0 pad_maximum_fusion
  51.5 94.5 %all-gather.5.cloned.1.call-done = f32[256,2,7168]{2,0,1:T(8,128)} async-done(((f32[64,2,7168]{2,0,1:T(8,128)}), f32[256,2,7168]{2,0,1:T(8,128)}) %all-gather.5.cloned.1.call-update) | async-done | bytes 14680080 | tf_op jit(solution)/shard_map/all_gather | solution.py:21
  145.9 8.4 %reduce_sum.56 = f32[64,2,7168]{2,0,1:T(8,128)} reduce(f32[4,64,2,7168]{3,1,0,2:T(8,128)} %bitcast.71, f32[]{:T(128)} %constant.13.clone.1), dimensions={0}, to_apply=%region_4.6 | reduce | flops 2752512 | bytes 18350084 | tf_op jit(solution)/shard_map/reduce_sum | solution.py:22
  154.4 16.4 %fusion.24 = bf16[64,2048]{1,0:T(8,128)(2,1)} fusion(bf16[1,7168,2048]{2,1,0:T(8,128)(2,1)} %param.14, f32[64,2,7168]{2,0,1:T(8,128)} %reduce_sum.56), kind=kOutput, calls=%fused_computation.22 | convolution fusion | flops 1881931776 | bytes 33292288 | tf_op jit(solution)/shard_map/dot_general | solution.py:25
  170.9 11.8 %reduce-scatter.3.cloned.1.call-done = bf16[32,2048]{1,0:T(8,128)(2,1)} async-done(((bf16[64,2048]{1,0:T(8,128)(2,1)}), bf16[32,2048]{1,0:T(8,128)(2,1)}) %reduce-scatter.3.cloned.1.call-update) | async-done | bytes 131088 | tf_op jit(solution)/shard_map/reduce_scatter | solution.py:24
  182.6 1.6 scatter_custom_fusion
  184.2 1.5 collective-permute-start
  185.7 14.0 %collective-permute-done = bf16[128,2048]{1,0:T(8,128)(2,1)S(1)} collective-permute-done((bf16[128,2048]{1,0:T(8,128)(2,1)S(1)}, bf16[128,2048]{1,0:T(8,128)(2,1)S(1)}, u32[]{:S(2)}, u32[]{:S(2)}) %collective-permute-start) | collective-permute-done | bytes 524320 | tf_op jit(solution)/shard_map/ppermute | solution.py:13
  200.6 5.7 %all-reduce = (f32[32]{0:T(128)S(1)}, f32[32]{0:T(128)S(1)}) all-reduce(f32[32]{0:T(128)S(1)} %get-tuple-element.7, f32[32]{0:T(128)S(1)} %get-tuple-element.6), channel_id=1, replica_groups=mesh['section'=4,'ctx'=4,'dp'=2] {'ctx'}, use_global_device_ids=true, to_apply=%region_10.12 | all-reduce | flops 64 | bytes 512 | tf_op jit(solution)/shard_map/psum | solution.py:38
  206.4 6.1 %all_gather.21 = bf16[64,2048]{1,0:T(8,128)(2,1)S(1)} all-gather(bf16[32,2048]{1,0:T(8,128)(2,1)S(1)} %fusion.46), channel_id=1, replica_groups=mesh['section'=4,'ctx'=4,'dp'=2] {'dp'}, dimensions={0}, use_global_device_ids=true | all-gather | bytes 393216 | tf_op jit(solution)/shard_map/all_gather | solution.py:17
  212.5 12.0 %fusion.15 = f32[64,1,7168]{2,0,1:T(8,128)S(1)} fusion(bf16[64,2048]{1,0:T(8,128)(2,1)S(1)} %all_gather.21, bf16[1,2048,7168]{2,1,0:T(8,128)(2,1)} %param.12), kind=kOutput, calls=%fused_computation.17 | convolution fusion | flops 1879048192 | bytes 31457280 | tf_op jit(solution)/shard_map/dot_general | solution.py:18
  224.5 12.0 %fusion.21 = f32[64,1,7168]{2,0,1:T(8,128)S(1)} fusion(bf16[64,2048]{1,0:T(8,128)(2,1)S(1)} %all_gather.21, bf16[1,2048,7168]{2,1,0:T(8,128)(2,1)} %param.13), kind=kOutput, calls=%fused_computation.19 | convolution fusion | flops 1879048192 | bytes 31457280 | tf_op jit(solution)/shard_map/dot_general | solution.py:19
  236.5 2.0 pad_maximum_fusion.1
  238.6 92.3 %all-gather.7.cloned.1.call-done = f32[256,2,7168]{2,0,1:T(8,128)} async-done(((f32[64,2,7168]{2,0,1:T(8,128)}), f32[256,2,7168]{2,0,1:T(8,128)}) %all-gather.7.cloned.1.call-update) | async-done | bytes 14680080 | tf_op jit(solution)/shard_map/all_gather | solution.py:21
  331.0 8.4 %reduce_sum.59 = f32[64,2,7168]{2,0,1:T(8,128)} reduce(f32[4,64,2,7168]{3,1,0,2:T(8,128)} %bitcast.70, f32[]{:T(128)} %constant.13.clone.1), dimensions={0}, to_apply=%region_11.13 | reduce | flops 2752512 | bytes 18350084 | tf_op jit(solution)/shard_map/reduce_sum | solution.py:22
  339.4 16.4 %fusion.27 = bf16[64,2048]{1,0:T(8,128)(2,1)} fusion(bf16[1,7168,2048]{2,1,0:T(8,128)(2,1)} %param.14, f32[64,2,7168]{2,0,1:T(8,128)} %reduce_sum.59), kind=kOutput, calls=%fused_computation.23 | convolution fusion | flops 1881931776 | bytes 33292288 | tf_op jit(solution)/shard_map/dot_general | solution.py:25
  355.9 11.8 %reduce-scatter.5.cloned.1.call-done = bf16[32,2048]{1,0:T(8,128)(2,1)} async-done(((bf16[64,2048]{1,0:T(8,128)(2,1)}), bf16[32,2048]{1,0:T(8,128)(2,1)}) %reduce-scatter.5.cloned.1.call-update) | async-done | bytes 131088 | tf_op jit(solution)/shard_map/reduce_scatter | solution.py:24
  367.6 1.6 scatter_custom_fusion.1
  369.2 0.9 select_bitcast_fusion
  (29 shorter events, 5.1 us)
Async XLA Ops:
  6.5 139.4 %all-gather.5.cloned.1.call-start = ((), (), s32[]{:S(2)}) async-start(), calls=%async_computation.4 | async-start | bytes 18350080 | tf_op jit(solution)/shard_map/all_gather | solution.py:21
  51.4 131.2 %reduce-scatter.3.cloned.1.call-start = ((), (), s32[]{:S(2)}) async-start(), calls=%async_computation.2 | async-start | bytes 393216 | tf_op jit(solution)/shard_map/reduce_scatter | solution.py:24
  154.4 16.5 %copy-start.1 = (s32[2,1,1,32]{3,2,1,0:T(1,128)S(1)}, s32[2,1,1,32]{3,2,1,0:T(1,128)}, u32[]{:S(2)}) copy-start(s32[2,1,1,32]{3,2,1,0:T(1,128)} %param.15) | copy-start | bytes 772
  154.4 51.9 %copy-start = (f32[1,2048]{1,0:T(1,128)S(1)}, f32[1,2048]{1,0:T(1,128)}, u32[]{:S(2)}) copy-start(f32[1,2048]{1,0:T(1,128)} %param.10) | copy-start | bytes 24580
  170.8 160.2 %all-gather.7.cloned.1.call-start = ((), (), s32[]{:S(2)}) async-start(), calls=%async_computation.5 | async-start | bytes 18350080 | tf_op jit(solution)/shard_map/all_gather | solution.py:21
  184.2 15.5 %collective-permute-start = (bf16[128,2048]{1,0:T(8,128)(2,1)S(1)}, bf16[128,2048]{1,0:T(8,128)(2,1)S(1)}, u32[]{:S(2)}, u32[]{:S(2)}) collective-permute-start(bf16[128,2048]{1,0:T(8,128)(2,1)S(1)} %scatter_custom_fusion), channel_id=1, source_target_pairs={{0,8},{8,16},{16,24},{24,0},{1,9},{9,17},{17,25},{25,1},{2,10},{10... | collective-permute-start | bytes 1572872 | tf_op jit(solution)/shard_map/ppermute | solution.py:13
  238.6 129.1 %reduce-scatter.5.cloned.1.call-start = ((), (), s32[]{:S(2)}) async-start(), calls=%async_computation.3 | async-start | bytes 393216 | tf_op jit(solution)/shard_map/reduce_scatter | solution.py:24
Sparse Core Ops, SparseCore 0:
  51.5 94.3 all-gather.4
  170.9 11.6 reduce-scatter.2
  238.7 92.2 all-gather.6
  355.9 11.6 reduce-scatter.4
